TPU v7x, 32 devices: a whole 2x2x4 slice. The times are simulated.
32 devices in a mesh: grp: 1, kz: 32 (over z, y, x, core).
Axes of the slice: x: 2, y: 2, z: 4, core: 2. Of those that a mesh axis runs over, the one named last changes fastest.
Arguments:
- kspace: float32 [8, 16, 512, 512], P('grp', None, 'kz'), may hold values from -8 to 8
- sensitivity: float32 [2, 256, 8, 16, 512], P(None, ('grp', 'kz')), may hold values from -2 to 2
- weight_first: bfloat16 [24, 2, 3, 3, 3], replicated, may hold values from -0.875 to 0.875
- bias_first: float32 [24], replicated, may hold values from -0.5 to 0.5
- weight_second: bfloat16 [24, 24, 3, 3, 3], replicated, may hold values from -0.3125 to 0.3125
- bias_second: float32 [24], replicated, may hold values from -0.5 to 0.5
- weight_third: bfloat16 [24, 24, 3, 3, 3], replicated, may hold values from -0.3125 to 0.3125
- bias_third: float32 [24], replicated, may hold values from -0.5 to 0.5
Outputs:
- features: bfloat16 [24, 512, 16, 256], P('grp', 'kz')
All inputs are finite; a program needn't handle non-finite values.
Results may differ from a plain program's by a relative error of at most 0.0058.
Values may be sent and summed in bfloat16 or wider, within the bound.
No kernel may reach another device: no remote copies, remote signals or barrier semaphores. Data moves between devices by JAX's collectives and lax.ppermute only.
A program may use at most 192 MiB of HBM per device.

v0:
```python
import math
import jax
import jax.numpy as jnp
from jax import lax
from jax.sharding import PartitionSpec as P

HIGHEST_PRECISION = lax.Precision.HIGHEST


def padded(x, sides, width):
    for axis, dim in sides:
        peers, length = (lax.axis_size(axis), x.shape[dim])
        up = [(i, (i + 1) % peers) for i in range(peers - 1)]
        down = [(j, i) for i, j in up]
        last = lax.slice_in_dim(x, length - width, length, axis=dim)
        first = lax.slice_in_dim(x, 0, width, axis=dim)
        before = lax.ppermute(last, axis, up)
        after = lax.ppermute(first, axis, down)
        x = jnp.concatenate([before, x, after], axis=dim)
    return x


def dft_parts(length):
    positions = jnp.arange(length, dtype=jnp.int32)
    phase_int = positions[:, None] * positions[None, :] % length
    angles = phase_int.astype(jnp.float32) * (2.0 * math.pi / length)
    factor = 1.0 / math.sqrt(length)
    return (jnp.cos(angles) * factor, jnp.sin(angles) * factor)


def y_table(length):
    cosine, sine_part = dft_parts(length)
    upper = jnp.concatenate([cosine, sine_part], axis=1)
    lower = jnp.concatenate([-sine_part, cosine], axis=1)
    return jnp.concatenate([upper, lower], axis=0)


def z_stacked(length):
    cosine, sine_part = dft_parts(length)
    from_real = jnp.stack([cosine, sine_part], axis=1)
    from_imag = jnp.stack([-sine_part, cosine], axis=1)
    return jnp.stack([from_real, from_imag], axis=1).reshape(2 * length, 2 * length)


def convolve(volume, weight, bias_vec):
    result = lax.conv_general_dilated(
        volume[None],
        weight,
        (1, 1, 1),
        [(0, 0), (1, 1), (1, 1)],
        dimension_numbers=("NCDHW", "OIDHW", "NCDHW"),
        preferred_element_type=jnp.float32,
    )[0]
    return jnp.maximum(result + bias_vec[:, None, None, None], 0.0)


def on_device(
    kspace,
    sensitivity,
    weight_first,
    bias_first,
    weight_second,
    bias_second,
    weight_third,
    bias_third,
):
    coil_count, rows_x, kz_local, twice_y = kspace.shape
    y_count = twice_y // 2
    kz_count = kz_local * lax.axis_size("kz")
    flat = kspace.reshape(-1, twice_y)
    y_lines = jnp.dot(
        flat, y_table(y_count), precision=HIGHEST_PRECISION, preferred_element_type=jnp.float32
    )
    y_lines = y_lines.reshape(coil_count, rows_x, kz_local, 2, y_count)
    z_matrix = z_stacked(kz_count)
    pieces = lax.all_to_all(y_lines, "kz", split_axis=4, concat_axis=2, tiled=True)
    coils_here, rows_here, kz_all, parts_here, y_here = pieces.shape
    grouped = pieces.reshape(coils_here * rows_here, kz_all * parts_here, y_here)
    product = lax.dot_general(
        grouped,
        z_matrix,
        (((1,), (0,)), ((), ())),
        precision=HIGHEST_PRECISION,
        preferred_element_type=jnp.float32,
    )
    coil_images = product.reshape(coils_here, rows_here, y_here, 2, kz_all)
    sens_view = jnp.transpose(sensitivity, (0, 2, 3, 1, 4))
    sens_re = sens_view[0]
    sens_im = sens_view[1]
    coil_re = coil_images[:, :, :, 0]
    coil_im = coil_images[:, :, :, 1]
    merged_re = jnp.sum(sens_re * coil_re + sens_im * coil_im, axis=0)
    merged_im = jnp.sum(sens_re * coil_im - sens_im * coil_re, axis=0)
    merged = jnp.stack([merged_re, merged_im], axis=0).astype(jnp.bfloat16)
    gathered = lax.all_to_all(merged, "kz", split_axis=3, concat_axis=2, tiled=True)
    slices = jnp.transpose(gathered, (0, 3, 1, 2))
    layers = ((weight_first, bias_first), (weight_second, bias_second), (weight_third, bias_third))
    activity = slices
    for weight, bias_vec in layers:
        extended = padded(activity, (("kz", 1),), 1)
        activity = convolve(extended, weight, bias_vec).astype(jnp.bfloat16)
    return activity


def solution(mesh):
    in_specs = (
        P("grp", None, "kz", None),
        P(None, ("grp", "kz"), None, None, None),
        P(),
        P(),
        P(),
        P(),
        P(),
        P(),
    )
    out_specs = P("grp", "kz", None, None)
    return jax.shard_map(
        on_device, mesh=mesh, in_specs=in_specs, out_specs=out_specs, check_vma=False
    )
```

profile of v0, /device:TPU:7, one launch (start us, length us, event | category | flops | bytes accessed | tf_op | source)
XLA Modules:
  0.0 860.8 jit_solution(986464142390691730)
XLA Ops:
  2.0 16.8 %convolution_bitcast_fusion = f32[2048,512]{0,1:T(8,128)} fusion(f32[2048,512]{1,0:T(8,128)} %bitcast.175, f32[256,256]{1,0:T(8,128)S(1)} %get-tuple-element.16, f32[256,256]{1,0:T(8,128)S(1)} %fusion.55, f32[256,256]{1,0:T(8,128)S(1)} %get-tuple-element.15), kind=kOutput, calls=%fused_computation.39 | convolution fusion | flops 6443237376 | bytes 9175040 | tf_op jit(solution)/shard_map/dot_general | solution.py:71
  30.1 26.3 %copy.113 = f32[8,16,16,2,256]{2,1,3,0,4:T(8,128)} copy(f32[8,16,16,2,256]{4,3,2,1,0:T(2,128)} %reshape.101) | data formatting | bytes 8388608 | tf_op jit(solution)/shard_map/reshape | solution.py:74
  56.4 29.0 %reshape.144 = f32[32,1,32768]{2,1,0:T(1,128)} reshape(f32[256,8,2,16,16]{4,3,2,1,0:T(8,128)} %bitcast.163) | data formatting | bytes 8388608
  120.8 64.2 %all-to-all-done = f32[32,1,32768]{2,1,0:T(1,128)} async-done(((f32[32,1,32768]{2,1,0:T(1,128)}), f32[32,1,32768]{2,1,0:T(1,128)}, u32[]{:S(2)}, u32[]{:S(2)}) %all-to-all-start) | async-done | bytes 4194336 | tf_op jit(solution)/shard_map/all_to_all | solution.py:76
  185.5 14.5 %reduce = f32[32,32768]{1,0:T(8,128)} reduce(f32[32,1,32768]{2,1,0:T(1,128)} %all-to-all-done, f32[]{:T(128)} %broadcast.231), dimensions={1}, to_apply=%all_to_all.24.reduce_sub_computation | reduce | bytes 8388612 | tf_op jit(solution)/shard_map/all_to_all | solution.py:76
  200.0 28.9 %reshape.145 = f32[256,8,2,16,16]{4,3,2,1,0:T(8,128)} reshape(f32[32,32768]{1,0:T(8,128)} %reduce) | data formatting | bytes 8388608
  228.9 36.6 %copy.115 = f32[8,16,32,16,2,8]{1,0,5,4,3,2:T(8,128)} copy(f32[8,16,32,16,2,8]{3,1,4,0,5,2:T(8,128)} %bitcast.164) | data formatting | bytes 8388608 | tf_op jit(solution)/shard_map/all_to_all | solution.py:76
  265.5 21.4 %reshape.102 = f32[128,1024,8]{0,2,1:T(8,128)} reshape(f32[8,16,32,16,2,8]{1,0,5,4,3,2:T(8,128)} %copy.115) | data formatting | bytes 8388608 | tf_op jit(solution)/shard_map/reshape | solution.py:78
  292.5 16.8 %fusion.69 = f32[8,16,8,2,512]{4,2,3,1,0:T(8,128)S(1)} fusion(f32[8,16,8,1024,1]{3,2,4,1,0:T(8,128)} %bitcast.174, f32[2,512,1024,1,1]{2,1,0,4,3:T(8,128)} %bitcast.173), kind=kOutput, calls=%fused_computation.97 | convolution fusion | flops 12884901888 | bytes 12582912 | tf_op jit(solution)/shard_map/dot_general | solution.py:79
  314.8 13.3 %all_to_all.33 = bf16[32,2,2048]{2,1,0:T(2,128)(2,1)S(1)} all-to-all(bf16[32,2,2048]{2,1,0:T(2,128)(2,1)S(1)} %reshape.146), channel_id=1, replica_groups=mesh['grp'=1,'kz'=32] {'kz'}, dimensions={0} | all-to-all | bytes 524288 | tf_op jit(solution)/shard_map/all_to_all | solution.py:95
  364.1 15.1 %fusion.82 = bf16[2,18,16,8,35]{3,0,4,2,1:T(2,128)(2,1)S(1)} fusion(bf16[2,18,16,1,7,2]{4,0,5,2,1,3:T(2,128)(2,1)S(1)} %slice.52, bf16[2,18,16,1,8,33]{4,0,5,2,1,3:T(2,128)(2,1)} %copy.127), kind=kLoop, calls=%fused_computation.34.clone.clone.1 | loop fusion | flops 967680 | bytes 642816 | tf_op jit(solution)/shard_map/conv_general_dilated | solution.py:46
  379.3 55.2 %convolution_select_fusion = f32[16,16,8,33,24]{4,2,3,1,0:T(8,128)} fusion(bf16[24,2,3,3,3]{0,1,4,3,2:T(2,128)(2,1)S(1)} %copy-done.7, pred[8,33]{0,1:T(8,128)(4,1)S(1)} %copy-done.8, bf16[2,18,16,8,35]{3,0,4,2,1:T(2,128)(2,1)S(1)} %fusion.82), kind=kOutput, calls=%fused_computation.16 | convolution fusion | flops 169500672 | bytes 6813480 | tf_op jit(solution)/shard_map/conv_general_dilated | solution.py:46
  434.5 32.2 %copy.128 = f32[16,16,8,33,24]{3,2,4,1,0:T(8,128)} copy(f32[16,16,8,33,24]{4,2,3,1,0:T(8,128)} %convolution_select_fusion) | data formatting | bytes 12976128 | tf_op jit(solution)/shard_map/conv_general_dilated | solution.py:46
  466.7 20.1 %reshape.110 = f32[16,16,1,264,24]{3,4,1,0,2:T(8,128)} reshape(f32[16,16,8,33,24]{3,2,4,1,0:T(8,128)} %copy.128) | data formatting | bytes 12976128 | tf_op jit(solution)/shard_map/conv_general_dilated | solution.py:46
  506.5 19.1 %reshape.142 = bf16[24,18,16,1,8,33]{5,4,0,2,1,3:T(8,128)(2,1)} reshape(bf16[24,18,16,1,264]{4,0,2,1,3:T(8,128)(2,1)} %pad.2) | data formatting | bytes 7299072 | tf_op jit(solution)/shard_map/conv_general_dilated | solution.py:46
  525.6 27.5 %copy.131 = bf16[24,18,16,1,8,33]{0,4,5,2,1,3:T(8,128)(2,1)} copy(bf16[24,18,16,1,8,33]{5,4,0,2,1,3:T(8,128)(2,1)} %reshape.142) | data formatting | bytes 7299072 | tf_op jit(solution)/shard_map/conv_general_dilated | solution.py:46
  554.8 63.6 %broadcast_select_fusion.1 = f32[16,16,8,33,24]{4,2,3,1,0:T(8,128)} fusion(pred[8,33]{0,1:T(8,128)(4,1)S(1)} %copy-done.8, bf16[24,24,3,3,3]{1,0,4,3,2:T(8,128)(2,1)S(1)} %copy-done, bf16[24,18,16,1,7,2]{0,4,5,2,1,3:T(8,128)(2,1)S(1)} %slice.56, bf16[24,18,16,1,8,33]{0,4,5,2,1,3:T(8,128)(2,1)} %copy.131), kind=kOutput, calls=%fused_computation.18 | convolution fusion | flops 2027778048 | bytes 10362504 | tf_op jit(solution)/shard_map/conv_general_dilated | solution.py:46
  618.3 32.0 %copy.132 = f32[16,16,8,33,24]{3,2,4,1,0:T(8,128)} copy(f32[16,16,8,33,24]{4,2,3,1,0:T(8,128)} %broadcast_select_fusion.1) | data formatting | bytes 12976128 | tf_op jit(solution)/shard_map/conv_general_dilated | solution.py:46
  650.4 20.1 %reshape.117 = f32[16,16,1,264,24]{3,4,1,0,2:T(8,128)} reshape(f32[16,16,8,33,24]{3,2,4,1,0:T(8,128)} %copy.132) | data formatting | bytes 12976128 | tf_op jit(solution)/shard_map/conv_general_dilated | solution.py:46
  690.4 19.1 %reshape.143 = bf16[24,18,16,1,8,33]{5,4,0,2,1,3:T(8,128)(2,1)} reshape(bf16[24,18,16,1,264]{4,0,2,1,3:T(8,128)(2,1)} %pad.4) | data formatting | bytes 7299072 | tf_op jit(solution)/shard_map/conv_general_dilated | solution.py:46
  709.5 27.5 %copy.135 = bf16[24,18,16,1,8,33]{0,4,5,2,1,3:T(8,128)(2,1)} copy(bf16[24,18,16,1,8,33]{5,4,0,2,1,3:T(8,128)(2,1)} %reshape.143) | data formatting | bytes 7299072 | tf_op jit(solution)/shard_map/conv_general_dilated | solution.py:46
  738.7 63.5 %broadcast_select_fusion = f32[16,16,8,33,24]{4,2,3,1,0:T(8,128)} fusion(pred[8,33]{0,1:T(8,128)(4,1)S(1)} %copy-done.8, bf16[24,24,3,3,3]{1,0,4,3,2:T(8,128)(2,1)S(1)} %copy-done.6, bf16[24,18,16,1,7,2]{0,4,5,2,1,3:T(8,128)(2,1)S(1)} %slice.60, bf16[24,18,16,1,8,33]{0,4,5,2,1,3:T(8,128)(2,1)} %copy.135), kind=kOutput, calls=%fused_computation.17 | convolution fusion | flops 2027778048 | bytes 10362504 | tf_op jit(solution)/shard_map/conv_general_dilated | solution.py:46
  802.2 32.0 %copy.136 = f32[16,16,8,33,24]{3,2,4,1,0:T(8,128)} copy(f32[16,16,8,33,24]{4,2,3,1,0:T(8,128)} %broadcast_select_fusion) | data formatting | bytes 12976128 | tf_op jit(solution)/shard_map/conv_general_dilated | solution.py:46
  834.3 20.1 %reshape.124 = f32[16,16,1,264,24]{3,4,1,0,2:T(8,128)} reshape(f32[16,16,8,33,24]{3,2,4,1,0:T(8,128)} %copy.136) | data formatting | bytes 12976128 | tf_op jit(solution)/shard_map/conv_general_dilated | solution.py:46
  (72 shorter events, 145.0 us)
Async XLA Ops:
  0.0 554.8 %copy-start = (bf16[24,24,3,3,3]{1,0,4,3,2:T(8,128)(2,1)S(1)}, bf16[24,24,3,3,3]{1,0,4,3,2:T(8,128)(2,1)}, u32[]{:S(2)}) copy-start(bf16[24,24,3,3,3]{1,0,4,3,2:T(8,128)(2,1)} %param.12) | copy-start | bytes 93316
  85.4 99.6 %all-to-all-start = ((f32[32,1,32768]{2,1,0:T(1,128)}), f32[32,1,32768]{2,1,0:T(1,128)}, u32[]{:S(2)}, u32[]{:S(2)}) async-start(f32[32,1,32768]{2,1,0:T(1,128)} %reshape.144), calls=%async_computation | async-start | bytes 8388608 | tf_op jit(solution)/shard_map/all_to_all | solution.py:76
  292.5 16.8 %copy-start.2 = (f32[2,8,8,16,512]{4,1,3,2,0:T(8,128)S(1)}, f32[2,8,8,16,512]{4,1,3,2,0:T(8,128)}, u32[]{:S(2)}) copy-start(f32[2,8,8,16,512]{4,1,3,2,0:T(8,128)} %copy.150) | copy-start | bytes 12582916
  339.3 9.2 %collective-permute-start = (bf16[2,1,16,256]{3,2,1,0:T(8,128)(2,1)S(1)}, bf16[2,1,16,256]{3,2,1,0:T(8,128)(2,1)S(1)}, u32[]{:S(2)}, u32[]{:S(2)}) collective-permute-start(bf16[2,1,16,256]{3,2,1,0:T(8,128)(2,1)S(1)} %copy.123), channel_id=1, source_target_pairs={{0,1},{1,2},{2,3},{3,4},{4,5},{5,6},{6,7},{7,8},{8,9},{9,10},{10,1... | collective-permute-start | bytes 49160 | tf_op jit(solution)/shard_map/ppermute | solution.py:17
  345.6 6.9 collective-permute-start.1
  364.1 15.1 %copy-start.7 = (bf16[24,2,3,3,3]{0,1,4,3,2:T(2,128)(2,1)S(1)}, bf16[24,2,3,3,3]{0,1,4,3,2:T(2,128)(2,1)}, u32[]{:S(2)}) copy-start(bf16[24,2,3,3,3]{0,1,4,3,2:T(2,128)(2,1)} %param.10) | copy-start | bytes 7780
  364.1 15.1 %copy-start.8 = (pred[8,33]{0,1:T(8,128)(4,1)S(1)}, pred[8,33]{0,1:T(8,128)(4,1)}, u32[]{:S(2)}) copy-start(pred[8,33]{0,1:T(8,128)(4,1)} %constant.54) | copy-start | bytes 796
  466.7 20.1 %copy-start.3 = (f32[24]{0:T(128)S(1)}, f32[24]{0:T(128)}, u32[]{:S(2)}) copy-start(f32[24]{0:T(128)} %param.11) | copy-start | bytes 292
  490.5 4.5 collective-permute-start.2
  492.4 8.8 %collective-permute-start.3 = (bf16[24,1,16,256]{3,0,2,1:T(8,128)(2,1)S(1)}, bf16[24,1,16,256]{3,0,2,1:T(8,128)(2,1)S(1)}, u32[]{:S(2)}, u32[]{:S(2)}) collective-permute-start(bf16[24,1,16,256]{3,0,2,1:T(8,128)(2,1)S(1)} %get-tuple-element.10), channel_id=1, source_target_pairs={{1,0},{2,1},{3,2},{4,3},{5,4},{6,5},{7,6},{8,7},{9,8},{10,9},{11,1... | collective-permute-start | bytes 589832 | tf_op jit(solution)/shard_map/ppermute | solution.py:18
  650.4 20.1 %copy-start.4 = (f32[24]{0:T(128)S(1)}, f32[24]{0:T(128)}, u32[]{:S(2)}) copy-start(f32[24]{0:T(128)} %param.13) | copy-start | bytes 292
  674.1 4.5 collective-permute-start.4
  676.1 8.8 %collective-permute-start.5 = (bf16[24,1,16,256]{3,0,2,1:T(8,128)(2,1)S(1)}, bf16[24,1,16,256]{3,0,2,1:T(8,128)(2,1)S(1)}, u32[]{:S(2)}, u32[]{:S(2)}) collective-permute-start(bf16[24,1,16,256]{3,0,2,1:T(8,128)(2,1)S(1)} %get-tuple-element.8), channel_id=1, source_target_pairs={{1,0},{2,1},{3,2},{4,3},{5,4},{6,5},{7,6},{8,7},{9,8},{10,9},{11,1... | collective-permute-start | bytes 589832 | tf_op jit(solution)/shard_map/ppermute | solution.py:18
  709.5 29.2 %copy-start.6 = (bf16[24,24,3,3,3]{1,0,4,3,2:T(8,128)(2,1)S(1)}, bf16[24,24,3,3,3]{1,0,4,3,2:T(8,128)(2,1)}, u32[]{:S(2)}) copy-start(bf16[24,24,3,3,3]{1,0,4,3,2:T(8,128)(2,1)} %param.14) | copy-start | bytes 93316
  834.3 20.1 %copy-start.5 = (f32[24]{0:T(128)S(1)}, f32[24]{0:T(128)}, u32[]{:S(2)}) copy-start(f32[24]{0:T(128)} %param.15) | copy-start | bytes 292
  854.4 6.0 copy-start.1
where the time goes:
time: 877 us; the launch traced here: 861 us
  local copies, waits for them, and re-layouts  475 us (54%)
  matrix products  216 us (25%)
  waiting for transfers between devices  81 us (9%)
  other arithmetic  53.8 us (6%)
  starting transfers between devices  21.6 us (2%)
  blocking collectives  13.3 us (2%)
    conv_general_dilated x15, local copies, waits for them, and re-layouts, convolve(): lax.conv_general_dilated(volume[None], weight, (1, 1, 1), [(0, 0), (1, 1)...  265 us
    conv_general_dilated x3, matrix products, convolve(): lax.conv_general_dilated(volume[None], weight, (1, 1, 1), [(0, 0), (1, 1)...  182 us
    unnamed x24, local copies, waits for them, and re-layouts  73.1 us
    all_to_all x1, waiting for transfers between devices, on_device(): lax.all_to_all(y_lines, 'kz', split_axis=4, concat_axis=2, tiled=True)  64.2 us
    all_to_all x2, local copies, waits for them, and re-layouts, on_device(): lax.all_to_all(y_lines, 'kz', split_axis=4, concat_axis=2, tiled=True)  37.1 us
    reshape x2, local copies, waits for them, and re-layouts, on_device(): y_lines = y_lines.reshape(coil_count, rows_x, kz_local, 2, y_count)  32.2 us
    reshape x1, local copies, waits for them, and re-layouts, on_device(): pieces.reshape(coils_here * rows_here, kz_all * parts_here, y_here)  21.4 us
  transfers between devices with their start and end apart: 7, of which 6 were waited for; matrix products, arithmetic and copies ran while one was open for 4% of the time, Pallas kernels for 0%

commit v1 on v0

--- a/solution.py
+++ b/solution.py
@@ -73,7 +73,10 @@
     )
     y_lines = y_lines.reshape(coil_count, rows_x, kz_local, 2, y_count)
     z_matrix = z_stacked(kz_count)
-    pieces = lax.all_to_all(y_lines, "kz", split_axis=4, concat_axis=2, tiled=True)
+    pieces = jnp.concatenate(
+        lax.all_to_all(jnp.stack(jnp.split(y_lines, lax.axis_size("kz"), axis=4)), "kz", 0, 0),
+        axis=2,
+    )
     coils_here, rows_here, kz_all, parts_here, y_here = pieces.shape
     grouped = pieces.reshape(coils_here * rows_here, kz_all * parts_here, y_here)
     product = lax.dot_general(

time: 877 us -> 1070 us (1.22)
  local copies, waits for them, and re-layouts: 475 us -> 670 us
    unnamed x24 -> x57, local copies, waits for them, and re-layouts: 73.1 us -> 185 us
    another operation x0 -> x3, local copies, waits for them, and re-layouts: none -> 108 us  [the longest x2 86.5 us: on_device(): jnp.stack(jnp.split(y_lines, lax.axis_size('kz'), axis=4))]
    reshape x1 -> x2, local copies, waits for them, and re-layouts: 21.4 us -> 60 us  [on_device(): jnp.concatenate(lax.all_to_all(jnp.stack(jnp.split(y_lines, lax.axis_size...]
    all_to_all x2 -> x1, local copies, waits for them, and re-layouts: 37.1 us -> 0.51 us  [on_device(): lax.all_to_all(jnp.stack(jnp.split(y_lines, lax.axis_size('kz'), axis=4))...]
    reshape x2 -> x1, local copies, waits for them, and re-layouts: 32.2 us -> 6.06 us  [on_device(): y_lines = y_lines.reshape(coil_count, rows_x, kz_local, 2, y_count)]
  transfers between devices with their start and end apart: 7 -> 7, of which waited for: 6 -> 6; matrix products, arithmetic and copies ran while one was open for 4% -> 3% of each run, Pallas kernels for 0% -> 0%
where the time goes in v1:
time: 1070 us; the launch traced here: 1060 us
  local copies, waits for them, and re-layouts  670 us (63%)
  matrix products  216 us (20%)
  waiting for transfers between devices  81 us (8%)
  other arithmetic  54 us (5%)
  starting transfers between devices  21.6 us (2%)
  blocking collectives  13.6 us (1%)
    conv_general_dilated x15, local copies, waits for them, and re-layouts, convolve(): lax.conv_general_dilated(volume[None], weight, (1, 1, 1), [(0, 0), (1, 1)...  265 us
    unnamed x57, local copies, waits for them, and re-layouts  185 us
    conv_general_dilated x3, matrix products, convolve(): lax.conv_general_dilated(volume[None], weight, (1, 1, 1), [(0, 0), (1, 1)...  182 us
    another operation x2, local copies, waits for them, and re-layouts, on_device(): jnp.stack(jnp.split(y_lines, lax.axis_size('kz'), axis=4))  86.5 us
    all_to_all x1, waiting for transfers between devices, on_device(): lax.all_to_all(jnp.stack(jnp.split(y_lines, lax.axis_size('kz'), axis=4))...  64.3 us
    reshape x2, local copies, waits for them, and re-layouts, on_device(): jnp.concatenate(lax.all_to_all(jnp.stack(jnp.split(y_lines, lax.axis_size...  60 us
    another operation x1, local copies, waits for them, and re-layouts, on_device(): pieces.reshape(coils_here * rows_here, kz_all * parts_here, y_here)  21.5 us
  transfers between devices with their start and end apart: 7, of which 6 were waited for; matrix products, arithmetic and copies ran while one was open for 3% of the time, Pallas kernels for 0%

profile of v1, /device:TPU:7, one launch (start us, length us, event | category | flops | bytes accessed | tf_op | source)
XLA Modules:
  0.0 1057.2 jit_solution(5250533626432726458)
XLA Ops:
  2.0 16.9 %convolution_bitcast_fusion = f32[2048,512]{0,1:T(8,128)} fusion(f32[2048,512]{1,0:T(8,128)} %bitcast.302, f32[256,256]{1,0:T(8,128)S(1)} %get-tuple-element.16, f32[256,256]{1,0:T(8,128)S(1)} %fusion.87, f32[256,256]{1,0:T(8,128)S(1)} %get-tuple-element.15), kind=kOutput, calls=%fused_computation.39 | convolution fusion | flops 6443237376 | bytes 9175040 | tf_op jit(solution)/shard_map/dot_general | solution.py:71
  145.7 83.0 %copy.152 = f32[32,8,16,16,2,8]{3,5,4,2,1,0:T(8,128)} copy(f32[32,8,16,16,2,8]{5,4,3,2,1,0:T(2,128)} %fusion.35) | data formatting | bytes 8388608 | tf_op jit(solution)/shard_map/stack | solution.py:77
  228.7 29.0 %reshape.143 = f32[32,1,32768]{2,1,0:T(1,128)} reshape(f32[32,8,16,2,8,16]{5,4,3,2,1,0:T(8,128)} %bitcast.291) | data formatting | bytes 8388608
  293.1 64.3 %all-to-all-done = f32[32,1,32768]{2,1,0:T(1,128)} async-done(((f32[32,1,32768]{2,1,0:T(1,128)}), f32[32,1,32768]{2,1,0:T(1,128)}, u32[]{:S(2)}, u32[]{:S(2)}) %all-to-all-start) | async-done | bytes 4194336 | tf_op jit(solution)/shard_map/all_to_all | solution.py:77
  357.9 14.4 %reduce = f32[32,32768]{1,0:T(8,128)} reduce(f32[32,1,32768]{2,1,0:T(1,128)} %all-to-all-done, f32[]{:T(128)} %broadcast.231), dimensions={1}, to_apply=%all_to_all.16.reduce_sub_computation | reduce | bytes 8388612 | tf_op jit(solution)/shard_map/all_to_all | solution.py:77
  372.3 28.9 %reshape.144 = f32[32,8,16,2,8,16]{5,4,3,2,1,0:T(8,128)} reshape(f32[32,32768]{1,0:T(8,128)} %reduce) | data formatting | bytes 8388608
  401.2 22.9 %bitcast_bitcast_fusion = f32[8,16,32,16,2,8]{3,5,4,1,0,2:T(8,128)} fusion(f32[32,8,16,2,8,16]{5,4,3,2,1,0:T(8,128)} %reshape.144), kind=kLoop, calls=%fused_computation.161 | loop fusion | bytes 8388608 | tf_op jit(solution)/shard_map/reshape | solution.py:76
  424.1 37.2 %copy.153 = f32[8,16,32,16,2,8]{1,0,5,4,3,2:T(8,128)} copy(f32[8,16,32,16,2,8]{3,5,4,1,0,2:T(8,128)} %bitcast_bitcast_fusion) | data formatting | bytes 8388608 | tf_op jit(solution)/shard_map/reshape | solution.py:76
  461.3 21.5 %reshape_reshape.3 = f32[128,1024,8]{0,2,1:T(8,128)} reshape(f32[8,16,32,16,2,8]{1,0,5,4,3,2:T(8,128)} %copy.153) | data formatting | bytes 8388608 | tf_op jit(solution)/shard_map/reshape;reshape | solution.py:81
  488.2 16.8 %fusion.101 = f32[8,16,8,2,512]{4,2,3,1,0:T(8,128)S(1)} fusion(f32[8,16,8,1024,1]{3,2,4,1,0:T(8,128)} %bitcast.301, f32[2,512,1024,1,1]{2,1,0,4,3:T(8,128)} %bitcast.300), kind=kOutput, calls=%fused_computation.162 | convolution fusion | flops 12884901888 | bytes 12582912 | tf_op jit(solution)/shard_map/dot_general | solution.py:82
  560.3 15.1 %fusion.114 = bf16[2,18,16,8,35]{3,0,4,2,1:T(2,128)(2,1)S(1)} fusion(bf16[2,18,16,1,7,2]{4,0,5,2,1,3:T(2,128)(2,1)S(1)} %slice.52, bf16[2,18,16,1,8,33]{4,0,5,2,1,3:T(2,128)(2,1)} %copy.165), kind=kLoop, calls=%fused_computation.34.clone.clone.1 | loop fusion | flops 967680 | bytes 642816 | tf_op jit(solution)/shard_map/conv_general_dilated | solution.py:46
  575.4 54.8 %convolution_select_fusion = f32[16,16,8,33,24]{4,2,3,1,0:T(8,128)} fusion(bf16[24,2,3,3,3]{0,1,4,3,2:T(2,128)(2,1)S(1)} %copy-done.8, pred[8,33]{0,1:T(8,128)(4,1)S(1)} %copy-done.9, bf16[2,18,16,8,35]{3,0,4,2,1:T(2,128)(2,1)S(1)} %fusion.114), kind=kOutput, calls=%fused_computation.16 | convolution fusion | flops 169500672 | bytes 6813480 | tf_op jit(solution)/shard_map/conv_general_dilated | solution.py:46
  630.3 32.2 %copy.166 = f32[16,16,8,33,24]{3,2,4,1,0:T(8,128)} copy(f32[16,16,8,33,24]{4,2,3,1,0:T(8,128)} %convolution_select_fusion) | data formatting | bytes 12976128 | tf_op jit(solution)/shard_map/conv_general_dilated | solution.py:46
  662.5 20.1 %reshape.109 = f32[16,16,1,264,24]{3,4,1,0,2:T(8,128)} reshape(f32[16,16,8,33,24]{3,2,4,1,0:T(8,128)} %copy.166) | data formatting | bytes 12976128 | tf_op jit(solution)/shard_map/conv_general_dilated | solution.py:46
  702.4 19.1 %reshape.141 = bf16[24,18,16,1,8,33]{5,4,0,2,1,3:T(8,128)(2,1)} reshape(bf16[24,18,16,1,264]{4,0,2,1,3:T(8,128)(2,1)} %pad.2) | data formatting | bytes 7299072 | tf_op jit(solution)/shard_map/conv_general_dilated | solution.py:46
  721.5 27.5 %copy.169 = bf16[24,18,16,1,8,33]{0,4,5,2,1,3:T(8,128)(2,1)} copy(bf16[24,18,16,1,8,33]{5,4,0,2,1,3:T(8,128)(2,1)} %reshape.141) | data formatting | bytes 7299072 | tf_op jit(solution)/shard_map/conv_general_dilated | solution.py:46
  750.7 63.7 %broadcast_select_fusion.1 = f32[16,16,8,33,24]{4,2,3,1,0:T(8,128)} fusion(pred[8,33]{0,1:T(8,128)(4,1)S(1)} %copy-done.9, bf16[24,24,3,3,3]{1,0,4,3,2:T(8,128)(2,1)S(1)} %copy-done, bf16[24,18,16,1,7,2]{0,4,5,2,1,3:T(8,128)(2,1)S(1)} %slice.56, bf16[24,18,16,1,8,33]{0,4,5,2,1,3:T(8,128)(2,1)} %copy.169), kind=kOutput, calls=%fused_computation.18 | convolution fusion | flops 2027778048 | bytes 10362504 | tf_op jit(solution)/shard_map/conv_general_dilated | solution.py:46
  814.4 32.0 %copy.170 = f32[16,16,8,33,24]{3,2,4,1,0:T(8,128)} copy(f32[16,16,8,33,24]{4,2,3,1,0:T(8,128)} %broadcast_select_fusion.1) | data formatting | bytes 12976128 | tf_op jit(solution)/shard_map/conv_general_dilated | solution.py:46
  846.4 20.1 %reshape.116 = f32[16,16,1,264,24]{3,4,1,0,2:T(8,128)} reshape(f32[16,16,8,33,24]{3,2,4,1,0:T(8,128)} %copy.170) | data formatting | bytes 12976128 | tf_op jit(solution)/shard_map/conv_general_dilated | solution.py:46
  886.6 19.1 %reshape.142 = bf16[24,18,16,1,8,33]{5,4,0,2,1,3:T(8,128)(2,1)} reshape(bf16[24,18,16,1,264]{4,0,2,1,3:T(8,128)(2,1)} %pad.4) | data formatting | bytes 7299072 | tf_op jit(solution)/shard_map/conv_general_dilated | solution.py:46
  905.7 27.5 %copy.173 = bf16[24,18,16,1,8,33]{0,4,5,2,1,3:T(8,128)(2,1)} copy(bf16[24,18,16,1,8,33]{5,4,0,2,1,3:T(8,128)(2,1)} %reshape.142) | data formatting | bytes 7299072 | tf_op jit(solution)/shard_map/conv_general_dilated | solution.py:46
  934.9 63.5 %broadcast_select_fusion = f32[16,16,8,33,24]{4,2,3,1,0:T(8,128)} fusion(pred[8,33]{0,1:T(8,128)(4,1)S(1)} %copy-done.9, bf16[24,24,3,3,3]{1,0,4,3,2:T(8,128)(2,1)S(1)} %copy-done.7, bf16[24,18,16,1,7,2]{0,4,5,2,1,3:T(8,128)(2,1)S(1)} %slice.60, bf16[24,18,16,1,8,33]{0,4,5,2,1,3:T(8,128)(2,1)} %copy.173), kind=kOutput, calls=%fused_computation.17 | convolution fusion | flops 2027778048 | bytes 10362504 | tf_op jit(solution)/shard_map/conv_general_dilated | solution.py:46
  998.4 32.0 %copy.174 = f32[16,16,8,33,24]{3,2,4,1,0:T(8,128)} copy(f32[16,16,8,33,24]{4,2,3,1,0:T(8,128)} %broadcast_select_fusion) | data formatting | bytes 12976128 | tf_op jit(solution)/shard_map/conv_general_dilated | solution.py:46
  1030.5 20.2 %reshape.123 = f32[16,16,1,264,24]{3,4,1,0,2:T(8,128)} reshape(f32[16,16,8,33,24]{3,2,4,1,0:T(8,128)} %copy.174) | data formatting | bytes 12976128 | tf_op jit(solution)/shard_map/conv_general_dilated | solution.py:46
  (107 shorter events, 274.3 us)
Async XLA Ops:
  0.0 750.7 %copy-start = (bf16[24,24,3,3,3]{1,0,4,3,2:T(8,128)(2,1)S(1)}, bf16[24,24,3,3,3]{1,0,4,3,2:T(8,128)(2,1)}, u32[]{:S(2)}) copy-start(bf16[24,24,3,3,3]{1,0,4,3,2:T(8,128)(2,1)} %param.12) | copy-start | bytes 93316
  30.4 8.4 copy-start.2
  257.8 99.6 %all-to-all-start = ((f32[32,1,32768]{2,1,0:T(1,128)}), f32[32,1,32768]{2,1,0:T(1,128)}, u32[]{:S(2)}, u32[]{:S(2)}) async-start(f32[32,1,32768]{2,1,0:T(1,128)} %reshape.143), calls=%async_computation | async-start | bytes 8388608 | tf_op jit(solution)/shard_map/all_to_all | solution.py:77
  488.2 16.8 %copy-start.3 = (f32[2,8,8,16,512]{4,1,3,2,0:T(8,128)S(1)}, f32[2,8,8,16,512]{4,1,3,2,0:T(8,128)}, u32[]{:S(2)}) copy-start(f32[2,8,8,16,512]{4,1,3,2,0:T(8,128)} %copy.187) | copy-start | bytes 12582916
  535.4 9.2 collective-permute-start
  541.8 6.9 collective-permute-start.1
  558.9 16.5 %copy-start.8 = (bf16[24,2,3,3,3]{0,1,4,3,2:T(2,128)(2,1)S(1)}, bf16[24,2,3,3,3]{0,1,4,3,2:T(2,128)(2,1)}, u32[]{:S(2)}) copy-start(bf16[24,2,3,3,3]{0,1,4,3,2:T(2,128)(2,1)} %param.10) | copy-start | bytes 7780
  558.9 16.5 %copy-start.9 = (pred[8,33]{0,1:T(8,128)(4,1)S(1)}, pred[8,33]{0,1:T(8,128)(4,1)}, u32[]{:S(2)}) copy-start(pred[8,33]{0,1:T(8,128)(4,1)} %constant.54) | copy-start | bytes 796
  662.5 20.2 %copy-start.4 = (f32[24]{0:T(128)S(1)}, f32[24]{0:T(128)}, u32[]{:S(2)}) copy-start(f32[24]{0:T(128)} %param.11) | copy-start | bytes 292
  686.4 4.5 collective-permute-start.2
  688.3 8.8 collective-permute-start.3
  846.4 20.2 %copy-start.5 = (f32[24]{0:T(128)S(1)}, f32[24]{0:T(128)}, u32[]{:S(2)}) copy-start(f32[24]{0:T(128)} %param.13) | copy-start | bytes 292
  870.3 4.5 collective-permute-start.4
  872.3 8.8 collective-permute-start.5
  905.7 29.2 %copy-start.7 = (bf16[24,24,3,3,3]{1,0,4,3,2:T(8,128)(2,1)S(1)}, bf16[24,24,3,3,3]{1,0,4,3,2:T(8,128)(2,1)}, u32[]{:S(2)}) copy-start(bf16[24,24,3,3,3]{1,0,4,3,2:T(8,128)(2,1)} %param.14) | copy-start | bytes 93316
  1030.5 20.2 %copy-start.6 = (f32[24]{0:T(128)S(1)}, f32[24]{0:T(128)}, u32[]{:S(2)}) copy-start(f32[24]{0:T(128)} %param.15) | copy-start | bytes 292
  1030.5 26.3 %copy-start.1 = (bf16[24,24,3,3,3]{1,0,4,3,2:T(8,128)(2,1)S(1)}, bf16[24,24,3,3,3]{1,0,4,3,2:T(8,128)(2,1)}, u32[]{:S(2)}) copy-start(bf16[24,24,3,3,3]{1,0,4,3,2:T(8,128)(2,1)} %param.12) | copy-start | bytes 93316
